TPU v7x, 768 devices: a whole 4x8x12 slice. The times are simulated.
768 devices in a mesh: node: 48 (over x, z), feat: 16 (over y, core).
Axes of the slice: x: 4, y: 8, z: 12, core: 2. Of those that a mesh axis runs over, the one named last changes fastest.
Arguments:
- features: bfloat16 [196608, 768], P('node', 'feat'), may hold values from -6 to 6
- req_local: int32 [48, 48, 256], P('node'), may hold values from 0 to 4095
- nbr_slot: int32 [24576, 25], P('node'), may hold values from 0 to 12287
- target_ids: int32 [24576], P('node'), may hold values from 0 to 4095
- w_self: bfloat16 [768, 1024], replicated, may hold values from -0.21875 to 0.21875
- w_neigh: bfloat16 [768, 1024], replicated, may hold values from -0.875 to 0.875
- bias_one: float32 [1024], P('feat'), may hold values from -3 to 3
- w_two: bfloat16 [1024, 1024], P(None, 'feat'), may hold values from -0.25 to 0.25
- bias_two: float32 [1024], P('feat'), may hold values from -3 to 3
Outputs:
- second_out: bfloat16 [24576, 1024], P('node', 'feat')
All inputs are finite; a program needn't handle non-finite values.
Results may differ from a plain program's by a relative error of at most 0.0052.
Values may be sent and summed in bfloat16 or wider, within the bound.
A program may use at most 64 MiB of HBM per device.

v0:
```python
import jax
import jax.numpy as jnp
from jax import lax
from jax.sharding import PartitionSpec as P

FAN = 25


def local(features, req_local, nbr_slot, target_ids, w_self, w_neigh, bias_one, w_two, bias_two):
    group = lax.axis_index("feat")
    columns = features.shape[1]
    wanted = req_local[0]
    served = lax.all_to_all(wanted, "node", split_axis=0, concat_axis=0, tiled=True)
    lookup = features[served]
    fetched = lax.all_to_all(lookup, "node", split_axis=0, concat_axis=0, tiled=True)
    buffer = fetched.reshape(-1, columns)
    picked = buffer[nbr_slot].astype(jnp.float32)
    neigh_mean = (jnp.sum(picked, axis=1) / FAN).astype(jnp.bfloat16)
    own = features[target_ids]
    self_rows = lax.dynamic_slice_in_dim(w_self, group * columns, columns, 0)
    neigh_rows = lax.dynamic_slice_in_dim(w_neigh, group * columns, columns, 0)
    partial_value = jnp.dot(own, self_rows, preferred_element_type=jnp.float32)
    partial_value = partial_value + jnp.dot(
        neigh_mean, neigh_rows, preferred_element_type=jnp.float32
    )
    pre = lax.psum_scatter(partial_value, "feat", scatter_dimension=1, tiled=True) + bias_one
    hidden_one = jnp.maximum(pre, 0.0).astype(jnp.bfloat16)
    second = jnp.dot(
        lax.all_gather(hidden_one, "feat", axis=1, tiled=True),
        w_two,
        preferred_element_type=jnp.float32,
    )
    result = (second + bias_two).astype(jnp.bfloat16)
    return result


def solution(mesh):
    placed = (
        P("node", "feat"),
        P("node", None, None),
        P("node", None),
        P("node"),
        P(),
        P(),
        P("feat"),
        P(None, "feat"),
        P("feat"),
    )
    return jax.shard_map(
        local, mesh=mesh, in_specs=placed, out_specs=P("node", "feat"), check_vma=False
    )
```

profile of v0, /device:TPU:1, one launch (start us, length us, event | category | flops | bytes accessed | tf_op | source)
XLA Modules:
  0.0 297.3 jit_solution(6827063568523763133)
XLA Ops:
  6.5 0.0 copy-start
  6.5 1.6 all_to_all.11
  8.1 18.8 %all-to-all-start = ((s32[48,1,256]{2,1,0:T(1,128)}), s32[48,1,256]{2,1,0:T(1,128)S(1)}, u32[]{:S(2)}, u32[]{:S(2)}) async-start(s32[48,1,256]{2,1,0:T(1,128)} %all_to_all.11), calls=%async_computation | async-start | bytes 98304 | tf_op jit(solution)/shard_map/all_to_all | solution.py:13
  27.0 1.5 copy.22
  28.4 9.9 %all-to-all-done = s32[48,1,256]{2,1,0:T(1,128)S(1)} async-done(((s32[48,1,256]{2,1,0:T(1,128)}), s32[48,1,256]{2,1,0:T(1,128)S(1)}, u32[]{:S(2)}, u32[]{:S(2)}) %all-to-all-start) | async-done | bytes 49184 | tf_op jit(solution)/shard_map/all_to_all | solution.py:13
  38.3 0.1 compare_select_fusion
  38.4 43.6 %gather_fusion.1 = bf16[12288,48]{1,0:T(8,128)(2,1)} fusion(bf16[4096,48]{1,0:T(8,128)(2,1)S(1)} %copy.22, s32[12288]{0:T(1024)S(1)} %broadcast_clamp_fusion), kind=kCustom, calls=%fused_computation.1 | custom fusion | bytes 2408448 | tf_op jit(solution)/shard_map/gather | solution.py:14
  82.0 4.1 %copy.24 = bf16[48,256,48]{1,2,0:T(8,128)(2,1)} copy(bf16[48,256,48]{2,1,0:T(8,128)(2,1)} %bitcast.17) | data formatting | bytes 2359296 | tf_op jit(solution)/shard_map/gather | solution.py:14
  86.1 0.0 copy-start.2
  86.1 0.0 copy-start.3
  86.1 5.5 %all-to-all-start.1 = ((bf16[48,256,48]{1,2,0:T(8,128)(2,1)}), bf16[48,256,48]{1,2,0:T(8,128)(2,1)}, u32[]{:S(2)}, u32[]{:S(2)}) async-start(bf16[48,256,48]{1,2,0:T(8,128)(2,1)} %copy.24), calls=%async_computation.1 | async-start | bytes 2359296 | tf_op jit(solution)/shard_map/all_to_all | solution.py:15
  91.6 0.0 reduce-scatter.4.cloned.1.call-start
  91.7 0.0 copy-done.2
  91.7 0.1 copy.26
  91.9 0.2 reshape.55
  92.1 0.0 copy-done.3
  92.1 1.3 gather_fusion
  93.5 0.0 copy-done
  93.5 1.9 fusion.5
  95.5 35.9 %all-to-all-done.1 = bf16[48,256,48]{1,2,0:T(8,128)(2,1)} async-done(((bf16[48,256,48]{1,2,0:T(8,128)(2,1)}), bf16[48,256,48]{1,2,0:T(8,128)(2,1)}, u32[]{:S(2)}, u32[]{:S(2)}) %all-to-all-start.1) | async-done | bytes 1179680 | tf_op jit(solution)/shard_map/all_to_all | solution.py:15
  131.3 3.9 %copy.25 = bf16[48,256,48]{2,1,0:T(8,128)(2,1)} copy(bf16[48,256,48]{1,2,0:T(8,128)(2,1)} %all-to-all-done.1) | data formatting | bytes 2359296 | tf_op jit(solution)/shard_map/all_to_all | solution.py:15
  135.3 26.6 %gather_fusion.2 = bf16[12800,48]{1,0:T(8,128)(2,1)} fusion(bf16[12288,48]{1,0:T(8,128)(2,1)} %bitcast.16, s32[13312]{0:T(1024)S(1)} %pad_clamp_fusion), kind=kCustom, calls=%fused_computation.2 | custom fusion | bytes 2508800 | tf_op jit(solution)/shard_map/gather | solution.py:17
  161.8 7.0 %reshape.65 = f32[512,25,48]{2,1,0:T(8,128)} reshape(bf16[12800,48]{1,0:T(8,128)(2,1)} %gather_fusion.2) | data formatting | bytes 3686400 | tf_op jit(solution)/shard_map/convert_element_type | solution.py:17
  168.8 5.2 %reduce_sum.9 = f32[512,48]{1,0:T(8,128)S(1)} reduce(f32[512,25,48]{2,1,0:T(8,128)} %reshape.65, f32[]{:T(128)} %constant.2.clone.1), dimensions={1}, to_apply=%region_0.0 | reduce | flops 589824 | bytes 2555908 | tf_op jit(solution)/shard_map/reduce_sum | solution.py:18
  173.9 3.6 %add_bitcast_fusion = f32[1024,512]{1,0:T(8,128)} fusion(f32[512,1024]{0,1:T(8,128)} %fusion.5, f32[512,48]{1,0:T(8,128)S(1)} %reduce_sum.9, bf16[768,1024]{1,0:T(8,128)(2,1)} %param.14, s32[]{:T(128)S(6)} %select_n.21), kind=kOutput, calls=%fused_computation.3 | convolution fusion | flops 50905088 | bytes 4390916 | tf_op jit(solution)/shard_map/dot_general | solution.py:23
  177.5 0.0 copy-start.4
  177.5 0.0 copy-start.1
  177.5 0.0 copy-start.5
  177.5 0.0 reduce-scatter.4.cloned.1.call-update
  177.6 0.0 all-gather.2.cloned.1.call-start
  177.6 64.1 %reduce-scatter.4.cloned.1.call-done = f32[64,512]{1,0:T(8,128)} async-done(((f32[1024,512]{1,0:T(8,128)}), f32[64,512]{1,0:T(8,128)}) %reduce-scatter.4.cloned.1.call-update) | async-done | bytes 131088
  241.7 0.0 copy-done.4
  241.7 1.6 fusion.2
  243.4 0.0 all-gather.2.cloned.1.call-update
  243.4 44.9 %all-gather.2.cloned.1.call-done = bf16[512,1024]{0,1:T(8,128)(2,1)} async-done(((bf16[512,64]{0,1:T(8,128)(2,1)}), bf16[512,1024]{0,1:T(8,128)(2,1)}) %all-gather.2.cloned.1.call-update) | async-done | bytes 1048592 | tf_op jit(solution)/shard_map/all_gather | solution.py:29
  288.3 0.0 copy-done.1
  288.3 0.0 copy-done.5
  288.3 2.2 fusion
  (5 shorter events, 0.0 us)
Async XLA Ops:
  6.5 87.0 %copy-start = (bf16[768,1024]{1,0:T(8,128)(2,1)S(1)}, bf16[768,1024]{1,0:T(8,128)(2,1)}, u32[]{:S(2)}) copy-start(bf16[768,1024]{1,0:T(8,128)(2,1)} %param.13) | copy-start | bytes 4718596
  8.1 30.2 %all-to-all-start = ((s32[48,1,256]{2,1,0:T(1,128)}), s32[48,1,256]{2,1,0:T(1,128)S(1)}, u32[]{:S(2)}, u32[]{:S(2)}) async-start(s32[48,1,256]{2,1,0:T(1,128)} %all_to_all.11), calls=%async_computation | async-start | bytes 98304 | tf_op jit(solution)/shard_map/all_to_all | solution.py:13
  86.1 5.6 %copy-start.2 = (s32[512,25]{0,1:T(8,128)S(1)}, s32[512,25]{0,1:T(8,128)}, u32[]{:S(2)}) copy-start(s32[512,25]{0,1:T(8,128)} %param.11) | copy-start | bytes 153604
  86.1 6.0 %copy-start.3 = (s32[512]{0:T(512)S(1)}, s32[512]{0:T(512)}, u32[]{:S(2)}) copy-start(s32[512]{0:T(512)} %param.12) | copy-start | bytes 6148
  86.1 45.2 %all-to-all-start.1 = ((bf16[48,256,48]{1,2,0:T(8,128)(2,1)}), bf16[48,256,48]{1,2,0:T(8,128)(2,1)}, u32[]{:S(2)}, u32[]{:S(2)}) async-start(bf16[48,256,48]{1,2,0:T(8,128)(2,1)} %copy.24), calls=%async_computation.1 | async-start | bytes 2359296 | tf_op jit(solution)/shard_map/all_to_all | solution.py:15
  91.6 150.1 %reduce-scatter.4.cloned.1.call-start = ((), (), s32[]{:S(2)}) async-start(), calls=%async_computation.4 | async-start | bytes 2228224
  177.5 64.2 %copy-start.4 = (f32[64]{0:T(128)S(1)}, f32[64]{0:T(128)}, u32[]{:S(2)}) copy-start(f32[64]{0:T(128)} %param.15) | copy-start | bytes 772
  177.5 110.8 %copy-start.1 = (bf16[1024,64]{0,1:T(8,128)(2,1)S(1)}, bf16[1024,64]{0,1:T(8,128)(2,1)}, u32[]{:S(2)}) copy-start(bf16[1024,64]{0,1:T(8,128)(2,1)} %param.16) | copy-start | bytes 393220
  177.5 110.8 %copy-start.5 = (f32[64]{0:T(128)S(1)}, f32[64]{0:T(128)}, u32[]{:S(2)}) copy-start(f32[64]{0:T(128)} %param.17) | copy-start | bytes 772
  177.6 110.7 %all-gather.2.cloned.1.call-start = ((), (), s32[]{:S(2)}) async-start(), calls=%async_computation.3 | async-start | bytes 1114112 | tf_op jit(solution)/shard_map/all_gather | solution.py:29
Sparse Core Ops, SparseCore 0:
  177.7 64.0 reduce-scatter.3
  244.1 44.0 all-gather.1
where the time goes:
time: 298 us; the launch traced here: 297 us
  waiting for transfers between devices  155 us (52%)
  local copies, waits for them, and re-layouts  90 us (30%)
  starting transfers between devices  24.4 us (8%)
  between operations  13.5 us (5%)
  matrix products  7.68 us (3%)
  other arithmetic  6.86 us (2%)
    unnamed x3, waiting for transfers between devices  64.2 us
    gather x2, local copies, waits for them, and re-layouts, local(): lookup = features[served]  47.7 us
    all_gather x1, waiting for transfers between devices, local(): lax.all_gather(hidden_one, 'feat', axis=1, tiled=True)  44.9 us
    all_to_all x1, waiting for transfers between devices, local(): lax.all_to_all(lookup, 'node', split_axis=0, concat_axis=0, tiled=True)  35.9 us
    gather x1, local copies, waits for them, and re-layouts, local(): picked = buffer[nbr_slot].astype(jnp.float32)  26.6 us
    all_to_all x1, starting transfers between devices, local(): lax.all_to_all(wanted, 'node', split_axis=0, concat_axis=0, tiled=True)  18.8 us
    all_to_all x1, waiting for transfers between devices, local(): lax.all_to_all(wanted, 'node', split_axis=0, concat_axis=0, tiled=True)  9.89 us
    convert_element_type x1, local copies, waits for them, and re-layouts, local(): picked = buffer[nbr_slot].astype(jnp.float32)  6.95 us
  transfers between devices with their start and end apart: 4, of which 4 were waited for; matrix products, arithmetic and copies ran while one was open for 2% of the time, Pallas kernels for 0%

commit v1 on v0

v1 whole, which is shorter than its diff:
```python
import functools

import jax
import jax.numpy as jnp
from jax import lax
from jax.experimental import pallas as pl
from jax.experimental.pallas import tpu as pltpu
from jax.sharding import PartitionSpec as P

FAN = 25
RING_X = 4
F32 = jnp.float32
BF16 = jnp.bfloat16
NT = (((1,), (1,)), ((), ()))
TN = (((0,), (0,)), ((), ()))


def offset(k, ring_x, ring_z):
    pair, side = lax.div(k, 2), lax.rem(k, 2)
    along, dx = lax.div(pair, ring_x), lax.rem(pair, ring_x)
    dz = along + side * (ring_z - 1 - 2 * along)
    return dx, dz


def kernel(
    sizes,
    feat_ref, req_ref, nbr_ref, tgt_ref, ws_ref, wn_ref, b1_ref, w2_ref, b2_ref,
    out_ref,
    table, req_out, req_in, rows_out, rows_in, count, hi_all, lo_all, acc, mixed,
    weight, w2_all, bias_out, bias_in, x_in, y_out, y_in,
    req_ss, req_rs, row_ss, row_rs, w_sem, w2_ss, w2_rs, b_ss, b_rs, x_ss, x_rs, y_ss, y_rs,
):
    ring_x, ring_z, groups, cap, own_rows, targets, cols = sizes
    nodes = ring_x * ring_z
    blocks = own_rows // 256
    share = targets // groups
    hidden = groups * 64
    node, feat = lax.axis_index("node"), lax.axis_index("feat")
    my_x, my_z = lax.div(node, ring_z), lax.rem(node, ring_z)

    def ahead(k):
        dx, dz = offset(k, ring_x, ring_z)
        return lax.rem(my_x + dx, ring_x) * ring_z + lax.rem(my_z + dz, ring_z)

    def behind(k):
        dx, dz = offset(k, ring_x, ring_z)
        return lax.rem(my_x + ring_x - dx, ring_x) * ring_z + lax.rem(my_z + ring_z - dz, ring_z)

    def mate(k):
        return lax.rem(feat + k, groups)

    def node_copy(src, dst, ss, rs, peer):
        return pltpu.make_async_remote_copy(
            src_ref=src, dst_ref=dst, send_sem=ss, recv_sem=rs,
            device_id={"node": peer}, device_id_type=pl.DeviceIdType.MESH,
        )

    def feat_copy(src, dst, ss, rs, peer):
        return pltpu.make_async_remote_copy(
            src_ref=src, dst_ref=dst, send_sem=ss, recv_sem=rs,
            device_id={"feat": peer}, device_id_type=pl.DeviceIdType.MESH,
        )

    def loop(low, high, body):
        def step(k, carry):
            body(k)
            return carry

        lax.fori_loop(low, high, step, 0)

    barrier = pltpu.get_barrier_semaphore()
    loop(1, nodes, lambda k: pl.semaphore_signal(
        barrier, inc=1, device_id={"node": ahead(k)}, device_id_type=pl.DeviceIdType.MESH))
    loop(1, groups, lambda k: pl.semaphore_signal(
        barrier, inc=1, device_id={"feat": mate(k)}, device_id_type=pl.DeviceIdType.MESH))

    def weight_copies(j):
        src = pl.ds(pl.multiple_of(j * cols, cols), cols)
        yield pltpu.make_async_copy(wn_ref.at[src], weight.at[j, pl.ds(0, cols)], w_sem.at[j])
        yield pltpu.make_async_copy(ws_ref.at[src], weight.at[j, pl.ds(cols, cols)], w_sem.at[groups + j])

    for j in range(groups):
        for copy in weight_copies(j):
            copy.start()
    weight[:, pl.ds(2 * cols, 128 - 2 * cols), :] = jnp.zeros((groups, 128 - 2 * cols, hidden), BF16)

    for j in range(blocks):
        table[pl.ds(j * cols, cols), :] = feat_ref[:, pl.ds(j * 256, 256)]
    for j in range(nodes):
        req_out[j] = req_ref[pl.ds(j, 1), :]
    bias_out[...] = jnp.zeros_like(bias_out)
    bias_out[pl.ds(0, 1), pl.ds(0, 64)] = b1_ref[...]
    bias_out[pl.ds(1, 1), pl.ds(0, 64)] = b2_ref[...]
    bias_out[...] = bias_out[...] + pltpu.roll(bias_out[...], 64, 1)
    bias_in[feat] = bias_out[...]
    w2_all[feat] = w2_ref[...]
    req_in[node] = req_out[node]

    pl.semaphore_wait(barrier, nodes - 1 + groups - 1)

    def send_request(k):
        peer = behind(k)
        node_copy(req_out.at[peer], req_in.at[node], req_ss.at[peer], req_rs.at[node], peer).start()

    loop(1, nodes, send_request)

    def send_second(k):
        peer = mate(k)
        feat_copy(bias_out, bias_in.at[feat], b_ss.at[peer], b_rs.at[feat], peer).start()
        feat_copy(w2_ref, w2_all.at[feat], w2_ss.at[peer], w2_rs.at[feat], peer).start()

    loop(1, groups, send_second)

    def pick(index):
        block, within = lax.shift_right_logical(index, 8), lax.bitwise_and(index, 255)
        row = lax.broadcasted_iota(jnp.int32, (256, 256), 0)
        one_hot = jnp.where(row == within, 1.0, 0.0).astype(BF16)
        every = jnp.dot(table[...], one_hot, preferred_element_type=F32)
        found = every[0:cols]
        for j in range(1, blocks):
            found = jnp.where(block == j, every[j * cols:(j + 1) * cols], found)
        return found

    for j in range(targets // 256):
        own = pick(tgt_ref[:, pl.ds(j * 256, 256)])
        wide = jnp.concatenate(
            [jnp.zeros((cols, 256), F32), own, jnp.zeros((128 - 2 * cols, 256), F32)], axis=0)
        mixed[pl.ds(j * 256, 256), :] = wide.T.astype(BF16)

    def serve(k):
        peer = ahead(k)
        node_copy(req_out.at[peer], req_in.at[peer], req_ss.at[peer], req_rs.at[peer], peer).wait_recv()
        rows_out[peer] = pick(req_in[peer]).astype(BF16)
        node_copy(rows_out.at[peer], rows_in.at[node], row_ss.at[peer], row_rs.at[node], peer).start()

    rows_in[node] = pick(req_in[node]).astype(BF16)
    loop(1, nodes, serve)

    slots = nbr_ref[...]
    spread = jnp.where(
        lax.bitwise_and(lax.broadcasted_iota(jnp.int32, (FAN, 256), 1), 31)
        == lax.broadcasted_iota(jnp.int32, (FAN, 256), 0), 1.0, 0.0).astype(BF16)
    hi = lax.shift_right_logical(slots, 8).astype(F32).astype(BF16)
    lo = lax.bitwise_and(slots, 255).astype(F32).astype(BF16)
    hi_all[...] = lax.dot_general(hi, spread, TN, preferred_element_type=F32)
    lo_all[...] = lax.dot_general(lo, spread, TN, preferred_element_type=F32)

    def count_eight(first):
        lane = lax.broadcasted_iota(jnp.int32, (8, 256), 1)
        sub = lax.broadcasted_iota(jnp.int32, (8, 256), 0)
        mine = (lax.shift_right_logical(lane, 5) == sub) & (lax.bitwise_and(lane, 31) < FAN)
        part = pl.ds(pl.multiple_of(first, 8), 8)
        his = jnp.where(mine, hi_all[part, :], -1.0)
        los = jnp.sum(jnp.where(mine, lo_all[part, :], 0.0), axis=0, keepdims=True)
        left = jnp.concatenate([jnp.where(his == float(d), 1.0, 0.0) for d in range(nodes)], axis=0)
        row = lax.broadcasted_iota(jnp.int32, (256, 256), 0)
        right = jnp.where(row == los.astype(jnp.int32), 1.0, 0.0)
        both = lax.dot_general(left.astype(BF16), right.astype(BF16), NT, preferred_element_type=F32)
        return both.reshape(nodes, 8, 256)

    def count_sixteen(j):
        first = pl.multiple_of(j * 16, 16)
        both = jnp.concatenate([count_eight(first), count_eight(first + 8)], axis=1)
        count[:, pl.ds(first, 16), :] = both.astype(BF16)

    loop(0, targets // 16, count_sixteen)

    def add_owner(owner):
        acc[...] += lax.dot_general(count[owner], rows_in[owner], NT, preferred_element_type=F32)

    acc[...] = lax.dot_general(count[node], rows_in[node], NT, preferred_element_type=F32)

    def take(k):
        owner = behind(k)
        node_copy(rows_out.at[owner], rows_in.at[owner], row_ss.at[owner], row_rs.at[owner], owner).wait_recv()
        add_owner(owner)

    loop(1, nodes, take)
    mixed[:, pl.ds(0, cols)] = (acc[...] / FAN).astype(BF16)

    def part_of(peer):
        return mixed.at[pl.ds(pl.multiple_of(peer * share, share), share), :]

    def send_mixed(k):
        peer = mate(k)
        feat_copy(part_of(peer), x_in.at[feat], x_ss.at[peer], x_rs.at[feat], peer).start()

    loop(1, groups, send_mixed)
    x_in[feat] = mixed[pl.ds(pl.multiple_of(feat * share, share), share), :]

    def got_second(k):
        peer = mate(k)
        feat_copy(bias_out, bias_in.at[peer], b_ss.at[peer], b_rs.at[peer], peer).wait_recv()
        feat_copy(w2_ref, w2_all.at[peer], w2_ss.at[peer], w2_rs.at[peer], peer).wait_recv()

    loop(1, groups, got_second)
    for j in range(groups):
        for copy in weight_copies(j):
            copy.wait()

    low_half = lax.broadcasted_iota(jnp.int32, (1, 128), 1) < 64
    bias = [
        jnp.concatenate([
            jnp.where(low_half, bias_in[2 * j, pl.ds(r, 1), :], bias_in[2 * j + 1, pl.ds(r, 1), :])
            for j in range(groups // 2)], axis=1)
        for r in range(2)]

    def got_mixed(k):
        peer = mate(k)
        feat_copy(part_of(peer), x_in.at[peer], x_ss.at[peer], x_rs.at[peer], peer).wait_recv()

    loop(1, groups, got_mixed)

    x = jnp.concatenate([x_in[j] for j in range(groups)], axis=1)
    pre = jnp.dot(x, weight[...].reshape(groups * 128, hidden), preferred_element_type=F32) + bias[0]
    one = jnp.maximum(pre, 0.0).astype(BF16)
    two = lax.dot_general(one, w2_all[...].reshape(hidden, hidden), NT, preferred_element_type=F32) + bias[1]
    two = two.astype(BF16)
    for j in range(groups // 2):
        y_out[j] = two[:, j * 128:(j + 1) * 128]

    def send_second_out(k):
        peer = mate(k)
        feat_copy(y_out.at[lax.div(peer, 2)], y_in.at[feat], y_ss.at[peer], y_rs.at[feat], peer).start()

    loop(1, groups, send_second_out)
    y_in[feat] = y_out[lax.div(feat, 2)]

    def got_second_out(k):
        peer = mate(k)
        feat_copy(y_out.at[lax.div(peer, 2)], y_in.at[peer], y_ss.at[peer], y_rs.at[peer], peer).wait_recv()

    loop(1, groups, got_second_out)
    turned = y_in[...].reshape(targets, 128).astype(F32).T
    out_ref[...] = jnp.where(lax.rem(feat, 2) == 0, turned[0:64], turned[64:128]).astype(BF16)

    def node_sent(k):
        peer = ahead(k)
        node_copy(req_out.at[peer], req_in.at[peer], req_ss.at[peer], req_rs.at[peer], peer).wait_send()
        node_copy(rows_out.at[peer], rows_in.at[peer], row_ss.at[peer], row_rs.at[peer], peer).wait_send()

    loop(1, nodes, node_sent)

    def feat_sent(k):
        peer = mate(k)
        feat_copy(bias_out, bias_in.at[peer], b_ss.at[peer], b_rs.at[peer], peer).wait_send()
        feat_copy(w2_ref, w2_all.at[peer], w2_ss.at[peer], w2_rs.at[peer], peer).wait_send()
        feat_copy(part_of(peer), x_in.at[peer], x_ss.at[peer], x_rs.at[peer], peer).wait_send()
        feat_copy(y_out.at[lax.div(peer, 2)], y_in.at[peer], y_ss.at[peer], y_rs.at[peer], peer).wait_send()

    loop(1, groups, feat_sent)


def local(groups, ring_x, features, req_local, nbr_slot, target_ids, w_self, w_neigh, bias_one, w_two, bias_two):
    _, nodes, cap = req_local.shape
    own_rows, cols = features.shape
    targets = nbr_slot.shape[0]
    hidden = w_self.shape[1]
    share = targets // groups
    sizes = (ring_x, nodes // ring_x, groups, cap, own_rows, targets, cols)
    vmem = pl.BlockSpec(memory_space=pltpu.VMEM)
    hbm = pl.BlockSpec(memory_space=pl.ANY)
    dma = pltpu.SemaphoreType.DMA
    out = pl.pallas_call(
        functools.partial(kernel, sizes),
        out_shape=jax.ShapeDtypeStruct((64, targets), BF16),
        in_specs=[vmem, vmem, vmem, vmem, hbm, hbm, vmem, vmem, vmem],
        out_specs=vmem,
        scratch_shapes=[
            pltpu.VMEM((own_rows // 256 * cols, 256), BF16),
            pltpu.VMEM((nodes, 1, cap), jnp.int32),
            pltpu.VMEM((nodes, 1, cap), jnp.int32),
            pltpu.VMEM((nodes, cols, cap), BF16),
            pltpu.VMEM((nodes, cols, cap), BF16),
            pltpu.VMEM((nodes, targets, cap), BF16),
            pltpu.VMEM((targets, 256), F32),
            pltpu.VMEM((targets, 256), F32),
            pltpu.VMEM((targets, cols), F32),
            pltpu.VMEM((targets, 128), BF16),
            pltpu.VMEM((groups, 128, hidden), BF16),
            pltpu.VMEM((groups, 64, hidden), BF16),
            pltpu.VMEM((8, 128), F32),
            pltpu.VMEM((groups, 8, 128), F32),
            pltpu.VMEM((groups, share, 128), BF16),
            pltpu.VMEM((groups // 2, share, 128), BF16),
            pltpu.VMEM((groups, share, 128), BF16),
            dma((nodes,)), dma((nodes,)), dma((nodes,)), dma((nodes,)),
            dma((2 * groups,)),
            dma((groups,)), dma((groups,)), dma((groups,)), dma((groups,)),
            dma((groups,)), dma((groups,)), dma((groups,)), dma((groups,)),
        ],
        compiler_params=pltpu.CompilerParams(
            collective_id=0, has_side_effects=True, vmem_limit_bytes=56 * 1024 * 1024
        ),
    )(
        features.T, req_local[0], nbr_slot.T, target_ids[None, :], w_self, w_neigh,
        bias_one[None, :], w_two.T, bias_two[None, :],
    )
    return out.T


def solution(mesh):
    placed = (
        P("node", "feat"),
        P("node", None, None),
        P("node", None),
        P("node"),
        P(),
        P(),
        P("feat"),
        P(None, "feat"),
        P("feat"),
    )
    return jax.shard_map(
        functools.partial(local, mesh.shape["feat"], RING_X), mesh=mesh, in_specs=placed,
        out_specs=P("node", "feat"), check_vma=False,
    )
```

time: 298 us -> 90.1 us (0.30)
  waiting for transfers between devices: 155 us -> 0 us
  local copies, waits for them, and re-layouts: 90 us -> 1.47 us
  Pallas kernels: 0 us -> 88.4 us
  starting transfers between devices: 24.4 us -> 0 us
  between operations: 13.5 us -> 0.01 us
  matrix products: 7.68 us -> 0 us
  other arithmetic: 6.86 us -> 0 us
    pallas_call x0 -> x1, Pallas kernels: none -> 88.4 us  [local(): pl.pallas_call(functools.partial(kernel, sizes), out_shape=jax.ShapeDtype...]
    gather x4 -> x0, local copies, waits for them, and re-layouts: 75.6 us -> none  [the longest x2 47.7 us: local(): lookup = features[served]]
    unnamed x3 -> x0, waiting for transfers between devices: 64.2 us -> none
    all_to_all x2 -> x0, waiting for transfers between devices: 45.8 us -> none  [the longest x1 35.9 us: local(): lax.all_to_all(lookup, 'node', split_axis=0, concat_axis=0, tiled=True)]
    all_gather x1 -> x0, waiting for transfers between devices: 44.9 us -> none  [local(): lax.all_gather(hidden_one, 'feat', axis=1, tiled=True)]
    all_to_all x2 -> x0, starting transfers between devices: 24.3 us -> none  [the longest x1 18.8 us: local(): lax.all_to_all(wanted, 'node', split_axis=0, concat_axis=0, tiled=True)]
    dot_general x3 -> x0, matrix products: 7.68 us -> none  [the longest x1 3.59 us: local(): jnp.dot(neigh_mean, neigh_rows, preferred_element_type=jnp.float32)]
    convert_element_type x1 -> x0, local copies, waits for them, and re-layouts: 6.95 us -> none  [local(): picked = buffer[nbr_slot].astype(jnp.float32)]
  transfers between devices with their start and end apart: 4 -> 0, of which waited for: 4 -> 0; matrix products, arithmetic and copies ran while one was open for 2% -> 0% of each run, Pallas kernels for 0% -> 0%
where the time goes in v1:
time: 90.1 us; the launch traced here: 89.9 us
  Pallas kernels  88.4 us (98%)
  local copies, waits for them, and re-layouts  1.47 us (2%)
    pallas_call x1, Pallas kernels, local(): pl.pallas_call(functools.partial(kernel, sizes), out_shape=jax.ShapeDtype...  88.4 us

profile of v1, /device:TPU:1, one launch (start us, length us, event | category | flops | bytes accessed | tf_op | source)
XLA Modules:
  0.0 89.9 jit_solution(13443311257125222421)
XLA Ops:
  0.0 88.4 %shard_map.91 = bf16[64,512]{1,0:T(8,128)(2,1)} custom-call(bf16[48,4096]{1,0:T(8,128)(2,1)} %bitcast.8, s32[48,256]{1,0:T(8,128)} %bitcast.12, s32[25,512]{1,0:T(8,128)} %bitcast.11, s32[1,512]{1,0:T(1,128)} %bitcast.13, bf16[768,1024]{1,0:T(8,128)(2,1)} %ws_ref.1, bf16[768,1024]{1,0:T(8,128)(2,1)} %wn_ref.1, f32[1,64]{1,0:T(1,128)} %bitcast.14, ...), custom_call_target="tpu_custom_call" | custom-call | tf_op jit(solution)/shard_map/pallas_call | solution.py:264
  88.4 1.5 %copy.11 = bf16[512,64]{0,1:T(8,128)(2,1)} copy(bf16[512,64]{0,1:T(8,128)(2,1)} %bitcast.9) | data formatting | bytes 131072

commit v2 on v1

v2 whole, which is shorter than its diff:
```python
import functools

import jax
import jax.numpy as jnp
from jax import lax
from jax.experimental import pallas as pl
from jax.experimental.pallas import tpu as pltpu
from jax.sharding import PartitionSpec as P

FAN = 25
UNROLL = 2
RING_X = 4
F32 = jnp.float32
BF16 = jnp.bfloat16
NT = (((1,), (1,)), ((), ()))
TN = (((0,), (0,)), ((), ()))


def lists(ring_z):
    far = (ring_z // 2 - 1) // 2
    return far, ring_z // 2 - 1 - far


def kernel(
    sizes,
    feat_ref, req_ref, nbr_ref, tgt_ref, ws_ref, wn_ref, b1_ref, w2_ref, b2_ref,
    out_ref,
    table, req_out, req_in, far_out, far_in, near_out, near_in, far_count, near_count,
    nbr_in, his, los, far_sum, near_sum, opposite_sum, mixed,
    weight, w2_all, bias_out, bias_in, x_in, y_out, y_in,
    req_ss, req_rs, far_ss, far_rs, near_ss, near_rs, pair_ss, pair_rs, w_sem, w2_ss, w2_rs, on_ss, b_ss, b_rs, x_ss, x_rs, y_ss, y_rs,
):
    ring_x, ring_z, groups, cap, own_rows, targets, cols = sizes
    nodes = ring_x * ring_z
    blocks = own_rows // 256
    share = targets // groups
    hidden = groups * 64
    node, feat = lax.axis_index("node"), lax.axis_index("feat")
    my_x, my_z = lax.div(node, ring_z), lax.rem(node, ring_z)

    half = ring_z // 2
    far_reach, near_reach = lists(ring_z)
    far_steps, near_steps = 2 * far_reach + 1, 2 * near_reach + 1

    def at(dx, dz):
        z = my_z + dz
        z = jnp.where(z < 0, z + ring_z, jnp.where(z >= ring_z, z - ring_z, z))
        return lax.bitwise_and(my_x + ring_x + dx, ring_x - 1) * ring_z + z

    def place(p, steps):
        p = jnp.int32(p)
        step = steps - 1 - lax.shift_right_logical(p, ring_x.bit_length() - 1)
        ahead = lax.shift_right_logical(step + 1, 1)
        return lax.bitwise_and(p, ring_x - 1), jnp.where(lax.bitwise_and(step, 1) == 1, ahead, -ahead)

    opposite = at(0, half)

    def mate(k):
        return lax.bitwise_and(feat + k, groups - 1)

    sibling = feat + 1 - 2 * lax.bitwise_and(feat, 1)

    def same_core(k):
        return lax.bitwise_and(feat + 2 * k, groups - 1)

    def node_copy(src, dst, ss, rs, peer):
        return pltpu.make_async_remote_copy(
            src_ref=src, dst_ref=dst, send_sem=ss, recv_sem=rs,
            device_id={"node": peer}, device_id_type=pl.DeviceIdType.MESH,
        )

    def feat_copy(src, dst, ss, rs, peer):
        return pltpu.make_async_remote_copy(
            src_ref=src, dst_ref=dst, send_sem=ss, recv_sem=rs,
            device_id={"feat": peer}, device_id_type=pl.DeviceIdType.MESH,
        )

    def loop(low, high, body):
        def step(k, carry):
            body(k)
            return carry

        lax.fori_loop(low, high, step, 0)

    barrier = pltpu.get_barrier_semaphore()
    def greet(k):
        peer = node + k
        peer = jnp.where(peer >= nodes, peer - nodes, peer)
        pl.semaphore_signal(barrier, inc=1, device_id={"node": peer}, device_id_type=pl.DeviceIdType.MESH)

    loop(1, nodes, greet)
    loop(1, groups, lambda k: pl.semaphore_signal(
        barrier, inc=1, device_id={"feat": mate(k)}, device_id_type=pl.DeviceIdType.MESH))

    for j in range(nodes):
        req_out[j] = req_ref[pl.ds(j, 1), :]

    pl.semaphore_wait(barrier, nodes - 1 + groups - 1)

    def nbr_copy():
        return node_copy(nbr_ref, nbr_in, pair_ss.at[0], pair_rs.at[0], opposite)

    def sum_copy():
        return node_copy(far_sum, opposite_sum, pair_ss.at[1], pair_rs.at[1], opposite)

    def request_to(peer):
        return node_copy(req_out.at[peer], req_in.at[node], req_ss.at[peer], req_rs.at[node], peer)

    def request_from(peer):
        return node_copy(req_out.at[peer], req_in.at[peer], req_ss.at[peer], req_rs.at[peer], peer)

    def far_owner(p):
        dx, dz = place(p, far_steps)
        return at(-dx, half - dz)

    def near_owner(p):
        dx, dz = place(p, near_steps)
        return at(-dx, -dz)

    far_all, near_all = far_steps * ring_x, near_steps * ring_x
    near_self, far_self = near_all - ring_x, far_all - ring_x
    nbr_copy().start()
    loop(0, far_all, lambda p: request_to(far_owner(p)).start())
    loop(0, near_self, lambda p: request_to(near_owner(p)).start())
    loop(near_self + 1, near_all, lambda p: request_to(near_owner(p)).start())

    def weight_copies(j):
        src = pl.ds(pl.multiple_of(j * cols, cols), cols)
        yield pltpu.make_async_copy(wn_ref.at[src], weight.at[j, pl.ds(0, cols)], w_sem.at[j])
        yield pltpu.make_async_copy(ws_ref.at[src], weight.at[j, pl.ds(cols, cols)], w_sem.at[groups + j])

    for j in range(blocks):
        table[pl.ds(j * cols, cols), :] = feat_ref[:, pl.ds(j * 256, 256)]
    req_in[node] = req_out[node]
    bias_out[...] = jnp.zeros_like(bias_out)
    bias_out[pl.ds(0, 1), pl.ds(0, 64)] = b1_ref[...]
    bias_out[pl.ds(1, 1), pl.ds(0, 64)] = b2_ref[...]
    bias_out[...] = bias_out[...] + pltpu.roll(bias_out[...], 64, 1)

    def second_copy(k):
        peer = same_core(k)
        return feat_copy(w2_ref, w2_all.at[feat], w2_ss.at[peer], w2_rs.at[feat], peer)

    def second_here(k):
        peer = same_core(k)
        return feat_copy(w2_ref, w2_all.at[peer], w2_ss.at[peer], w2_rs.at[peer], peer)

    def second_on(k):
        source = same_core(k)
        return feat_copy(w2_all.at[source], w2_all.at[source], on_ss.at[k], w2_rs.at[source], sibling)

    def second_beside(k):
        source = lax.bitwise_and(sibling + 2 * k, groups - 1)
        return feat_copy(w2_all.at[source], w2_all.at[source], on_ss.at[k], w2_rs.at[source], sibling)

    def bias_copy(k):
        peer = mate(k)
        return feat_copy(bias_out, bias_in.at[feat], b_ss.at[peer], b_rs.at[feat], peer)

    def pick(index):
        block, within = lax.shift_right_logical(index, 8), lax.bitwise_and(index, 255)
        row = lax.broadcasted_iota(jnp.int32, (256, 256), 0)
        one_hot = jnp.where(row == within, 1.0, 0.0).astype(BF16)
        every = jnp.dot(table[...], one_hot, preferred_element_type=F32)
        found = every[0:cols]
        for j in range(1, blocks):
            found = jnp.where(block == j, every[j * cols:(j + 1) * cols], found)
        return found

    def far_copy(p):
        dx, dz = place(p, far_steps)
        return node_copy(far_out.at[p], far_in.at[p], far_ss.at[p], far_rs.at[p], at(dx, dz))

    def near_copy(p):
        dx, dz = place(p, near_steps)
        return node_copy(near_out.at[p], near_in.at[p], near_ss.at[p], near_rs.at[p], at(dx, dz))

    def far_asker(p):
        dx, dz = place(p, far_steps)
        return at(dx, dz + half)

    def near_asker(p):
        dx, dz = place(p, near_steps)
        return at(dx, dz)

    def serve(asker, out, copy, entries):
        askers = [asker(p) for p in entries]
        for peer in askers:
            request_from(peer).wait_recv()
        for p, peer in zip(entries, askers, strict=True):
            out[p] = pick(req_in[peer]).astype(BF16)
        for p in entries:
            copy(p).start()

    loop(0, far_self // 2, lambda k: serve(far_asker, far_out, far_copy, [2 * k, 2 * k + 1]))
    serve(far_asker, far_out, far_copy, range(far_self + 1, far_all))
    loop(1, groups // 2, lambda k: second_copy(k).start())
    loop(1, groups, lambda k: bias_copy(k).start())
    loop(0, near_self // 2, lambda k: serve(near_asker, near_out, near_copy, [2 * k, 2 * k + 1]))
    serve(near_asker, near_out, near_copy, range(near_self + 1, near_all))
    request_from(opposite).wait_recv()
    far_in[far_self] = pick(req_in[opposite]).astype(BF16)
    near_in[near_self] = pick(req_in[node]).astype(BF16)

    spread = jnp.where(
        lax.bitwise_and(lax.broadcasted_iota(jnp.int32, (FAN, 256), 1), 31)
        == lax.broadcasted_iota(jnp.int32, (FAN, 256), 0), 1.0, 0.0).astype(BF16)

    def spread_slots(slots, which):
        hi = lax.shift_right_logical(slots, 8).astype(F32).astype(BF16)
        lo = lax.bitwise_and(slots, 255).astype(F32).astype(BF16)
        his[which] = lax.dot_general(hi, spread, TN, preferred_element_type=F32)
        los[which] = lax.dot_general(lo, spread, TN, preferred_element_type=F32)

    def count_eight(which, owners, first):
        lane = lax.broadcasted_iota(jnp.int32, (8, 256), 1)
        sub = lax.broadcasted_iota(jnp.int32, (8, 256), 0)
        mine = (lax.shift_right_logical(lane, 5) == sub) & (lax.bitwise_and(lane, 31) < FAN)
        part = pl.ds(pl.multiple_of(first, 8), 8)
        hi = jnp.where(mine, his[which, part, :], -1.0)
        lo = jnp.sum(jnp.where(mine, los[which, part, :], 0.0), axis=0, keepdims=True)
        left = jnp.concatenate([jnp.where(hi == owner, 1.0, 0.0) for owner in owners], axis=0)
        row = lax.broadcasted_iota(jnp.int32, (256, 256), 0)
        right = jnp.where(row == lo.astype(jnp.int32), 1.0, 0.0)
        both = lax.dot_general(left.astype(BF16), right.astype(BF16), NT, preferred_element_type=F32)
        return both.reshape(len(owners), 8, 256)

    def count_some(which, count, owners, low, high):
        def body(k):
            for part in range(UNROLL):
                first = pl.multiple_of((k * UNROLL + part) * 16, 16)
                both = [count_eight(which, owners, first + 8 * i) for i in range(2)]
                count[:, pl.ds(first, 16), :] = jnp.concatenate(both, axis=1).astype(BF16)

        loop(low, high, body)

    def list_owners(steps):
        found = []
        for p in range(steps * ring_x):
            dx, dz = place(p, steps)
            found.append(at(-dx, -dz).astype(F32))
        return found

    turns = targets // (16 * UNROLL)
    nbr_copy().wait_recv()
    spread_slots(nbr_in[...], 1)
    count_some(1, far_count, list_owners(far_steps), 0, turns)

    def add_rows(total, count, rows, entries):
        for p in entries:
            total = total + lax.dot_general(rows[p], count[p], NT, preferred_element_type=F32)
        return total

    def take(copy, sums, count, rows, entries):
        for p in entries:
            copy(p).wait_recv()
        sums[...] = add_rows(sums[...], count, rows, entries)

    def take_all(copy, sums, count, rows, own):
        sums[...] = add_rows(jnp.zeros_like(sums), count, rows, [own])
        loop(0, own // ring_x, lambda k: take(
            copy, sums, count, rows, [ring_x * k + j for j in range(ring_x)]))
        take(copy, sums, count, rows, range(own + 1, own + ring_x))

    take_all(far_copy, far_sum, far_count, far_in, far_self)
    sum_copy().start()

    spread_slots(nbr_ref[...], 0)
    count_some(0, near_count, list_owners(near_steps), 0, turns)

    feat_copy(w2_ref, w2_all.at[feat], on_ss.at[0], w2_rs.at[feat], sibling).start()

    def second_forward(k):
        second_here(k).wait_recv()
        second_on(k).start()

    loop(1, groups // 2, second_forward)

    for j in range(targets // 256):
        own = pick(tgt_ref[:, pl.ds(j * 256, 256)])
        wide = jnp.concatenate(
            [jnp.zeros((cols, 256), F32), own, jnp.zeros((128 - 2 * cols, 256), F32)], axis=0)
        mixed[pl.ds(j * 256, 256), :] = wide.T.astype(BF16)

    for j in range(groups):
        for copy in weight_copies(j):
            copy.start()
    weight[:, pl.ds(2 * cols, 128 - 2 * cols), :] = jnp.zeros((groups, 128 - 2 * cols, hidden), BF16)
    bias_in[feat] = bias_out[...]
    w2_all[feat] = w2_ref[...]

    take_all(near_copy, near_sum, near_count, near_in, near_self)
    sum_copy().wait_recv()
    mean = (near_sum[...] + opposite_sum[...]) / FAN
    mean = jnp.concatenate([mean, jnp.zeros((128 - cols, targets), F32)], axis=0)
    mixed[:, pl.ds(0, cols)] = mean.T[:, 0:cols].astype(BF16)

    def part_of(peer):
        return mixed.at[pl.ds(pl.multiple_of(peer * share, share), share), :]

    def send_mixed(k):
        peer = mate(k)
        feat_copy(part_of(peer), x_in.at[feat], x_ss.at[peer], x_rs.at[feat], peer).start()

    loop(1, groups, send_mixed)
    x_in[feat] = mixed[pl.ds(pl.multiple_of(feat * share, share), share), :]

    def bias_here(k):
        peer = mate(k)
        return feat_copy(bias_out, bias_in.at[peer], b_ss.at[peer], b_rs.at[peer], peer)

    loop(1, groups, lambda k: bias_here(k).wait_recv())
    loop(0, groups // 2, lambda k: second_beside(k).wait_recv())

    loop(0, far_all, lambda p: request_to(far_owner(p)).wait_send())
    loop(0, near_self, lambda p: request_to(near_owner(p)).wait_send())
    loop(near_self + 1, near_all, lambda p: request_to(near_owner(p)).wait_send())
    loop(0, far_self, lambda p: far_copy(p).wait_send())
    loop(far_self + 1, far_all, lambda p: far_copy(p).wait_send())
    loop(0, near_self, lambda p: near_copy(p).wait_send())
    loop(near_self + 1, near_all, lambda p: near_copy(p).wait_send())
    nbr_copy().wait_send()
    sum_copy().wait_send()
    loop(1, groups // 2, lambda k: second_copy(k).wait_send())
    loop(0, groups // 2, lambda k: second_on(k).wait_send())
    loop(1, groups, lambda k: bias_copy(k).wait_send())
    for j in range(groups):
        for copy in weight_copies(j):
            copy.wait()

    low_half = lax.broadcasted_iota(jnp.int32, (1, 128), 1) < 64
    bias = [
        jnp.concatenate([
            jnp.where(low_half, bias_in[2 * j, pl.ds(r, 1), :], bias_in[2 * j + 1, pl.ds(r, 1), :])
            for j in range(groups // 2)], axis=1)
        for r in range(2)]

    def got_mixed(k):
        peer = mate(k)
        feat_copy(part_of(peer), x_in.at[peer], x_ss.at[peer], x_rs.at[peer], peer).wait_recv()

    loop(1, groups, got_mixed)

    x = jnp.concatenate([x_in[j] for j in range(groups)], axis=1)
    pre = jnp.dot(x, weight[...].reshape(groups * 128, hidden), preferred_element_type=F32) + bias[0]
    one = jnp.maximum(pre, 0.0).astype(BF16)
    two = lax.dot_general(one, w2_all[...].reshape(hidden, hidden), NT, preferred_element_type=F32) + bias[1]
    two = two.astype(BF16)
    for j in range(groups // 2):
        y_out[j] = two[:, j * 128:(j + 1) * 128]

    def send_second_out(k):
        peer = mate(k)
        feat_copy(y_out.at[lax.div(peer, 2)], y_in.at[feat], y_ss.at[peer], y_rs.at[feat], peer).start()

    loop(1, groups, send_second_out)
    y_in[feat] = y_out[lax.div(feat, 2)]

    def got_second_out(k):
        peer = mate(k)
        feat_copy(y_out.at[lax.div(peer, 2)], y_in.at[peer], y_ss.at[peer], y_rs.at[peer], peer).wait_recv()

    loop(1, groups, got_second_out)
    turned = y_in[...].reshape(targets, 128).astype(F32).T
    out_ref[...] = jnp.where(lax.rem(feat, 2) == 0, turned[0:64], turned[64:128]).astype(BF16)

    def feat_sent(k):
        peer = mate(k)
        feat_copy(part_of(peer), x_in.at[peer], x_ss.at[peer], x_rs.at[peer], peer).wait_send()
        feat_copy(y_out.at[lax.div(peer, 2)], y_in.at[peer], y_ss.at[peer], y_rs.at[peer], peer).wait_send()

    loop(1, groups, feat_sent)


def local(groups, ring_x, features, req_local, nbr_slot, target_ids, w_self, w_neigh, bias_one, w_two, bias_two):
    _, nodes, cap = req_local.shape
    own_rows, cols = features.shape
    targets = nbr_slot.shape[0]
    hidden = w_self.shape[1]
    share = targets // groups
    sizes = (ring_x, nodes // ring_x, groups, cap, own_rows, targets, cols)
    far, near = ((2 * reach + 1) * ring_x for reach in lists(nodes // ring_x))
    vmem = pl.BlockSpec(memory_space=pltpu.VMEM)
    hbm = pl.BlockSpec(memory_space=pl.ANY)
    dma = pltpu.SemaphoreType.DMA
    out = pl.pallas_call(
        functools.partial(kernel, sizes),
        out_shape=jax.ShapeDtypeStruct((64, targets), BF16),
        in_specs=[vmem, vmem, vmem, vmem, hbm, hbm, vmem, vmem, vmem],
        out_specs=vmem,
        scratch_shapes=[
            pltpu.VMEM((own_rows // 256 * cols, 256), BF16),
            pltpu.VMEM((nodes, 1, cap), jnp.int32),
            pltpu.VMEM((nodes, 1, cap), jnp.int32),
            pltpu.VMEM((far, cols, cap), BF16),
            pltpu.VMEM((far, cols, cap), BF16),
            pltpu.VMEM((near, cols, cap), BF16),
            pltpu.VMEM((near, cols, cap), BF16),
            pltpu.VMEM((far, targets, cap), BF16),
            pltpu.VMEM((near, targets, cap), BF16),
            pltpu.VMEM(nbr_slot.shape[::-1], jnp.int32),
            pltpu.VMEM((2, targets, 256), F32),
            pltpu.VMEM((2, targets, 256), F32),
            pltpu.VMEM((cols, targets), F32),
            pltpu.VMEM((cols, targets), F32),
            pltpu.VMEM((cols, targets), F32),
            pltpu.VMEM((targets, 128), BF16),
            pltpu.VMEM((groups, 128, hidden), BF16),
            pltpu.VMEM((groups, 64, hidden), BF16),
            pltpu.VMEM((8, 128), F32),
            pltpu.VMEM((groups, 8, 128), F32),
            pltpu.VMEM((groups, share, 128), BF16),
            pltpu.VMEM((groups // 2, share, 128), BF16),
            pltpu.VMEM((groups, share, 128), BF16),
            dma((nodes,)), dma((nodes,)), dma((far,)), dma((far,)), dma((near,)), dma((near,)), dma((2,)), dma((2,)),
            dma((2 * groups,)),
            dma((groups,)), dma((groups,)), dma((groups // 2,)), dma((groups,)), dma((groups,)),
            dma((groups,)), dma((groups,)), dma((groups,)), dma((groups,)),
        ],
        compiler_params=pltpu.CompilerParams(
            collective_id=0, has_side_effects=True, vmem_limit_bytes=56 * 1024 * 1024
        ),
    )(
        features.T, req_local[0], nbr_slot.T, target_ids[None, :], w_self, w_neigh,
        bias_one[None, :], w_two.T, bias_two[None, :],
    )
    return out.T


def solution(mesh):
    placed = (
        P("node", "feat"),
        P("node", None, None),
        P("node", None),
        P("node"),
        P(),
        P(),
        P("feat"),
        P(None, "feat"),
        P("feat"),
    )
    return jax.shard_map(
        functools.partial(local, mesh.shape["feat"], RING_X), mesh=mesh, in_specs=placed,
        out_specs=P("node", "feat"), check_vma=False,
    )
```

time: 90.1 us -> 83.3 us (0.925)
  Pallas kernels: 88.4 us -> 81.7 us
    pallas_call x1, Pallas kernels: 88.4 us -> 81.7 us  [local(): pl.pallas_call(functools.partial(kernel, sizes), out_shape=jax.ShapeDtype...]
where the time goes in v2:
time: 83.3 us; the launch traced here: 83.2 us
  Pallas kernels  81.7 us (98%)
  local copies, waits for them, and re-layouts  1.47 us (2%)
    pallas_call x1, Pallas kernels, local(): pl.pallas_call(functools.partial(kernel, sizes), out_shape=jax.ShapeDtype...  81.7 us

profile of v2, /device:TPU:1, one launch (start us, length us, event | category | flops | bytes accessed | tf_op | source)
XLA Modules:
  0.0 83.2 jit_solution(6917398164564097666)
XLA Ops:
  0.0 81.7 %shard_map.91 = bf16[64,512]{1,0:T(8,128)(2,1)} custom-call(bf16[48,4096]{1,0:T(8,128)(2,1)} %bitcast.8, s32[48,256]{1,0:T(8,128)} %bitcast.12, s32[25,512]{1,0:T(8,128)} %bitcast.11, s32[1,512]{1,0:T(1,128)} %bitcast.13, bf16[768,1024]{1,0:T(8,128)(2,1)} %ws_ref.1, bf16[768,1024]{1,0:T(8,128)(2,1)} %wn_ref.1, f32[1,64]{1,0:T(1,128)} %bitcast.14, ...), custom_call_target="tpu_custom_call" | custom-call | tf_op jit(solution)/shard_map/pallas_call | solution.py:386
  81.7 1.5 %copy.11 = bf16[512,64]{0,1:T(8,128)(2,1)} copy(bf16[512,64]{0,1:T(8,128)(2,1)} %bitcast.9) | data formatting | bytes 131072

commit v3 on v0

v3 whole, which is shorter than its diff:
```python
import functools

import jax
import jax.numpy as jnp
from jax import lax
from jax.experimental import pallas as pl
from jax.experimental.pallas import tpu as pltpu
from jax.sharding import PartitionSpec as P

FAN = 25
RING_X = 4
UNROLL = 4
F32 = jnp.float32
BF16 = jnp.bfloat16
PARTIAL = BF16
EARLY = 4
MESH = pl.DeviceIdType.MESH
NT = (((1,), (1,)), ((), ()))
TN = (((0,), (0,)), ((), ()))


def lists(ring_z):
    far = (ring_z // 2 - 1) // 2
    return far, ring_z // 2 - 1 - far


def kernel(
    sizes,
    feat_hbm, req_hbm, nbr_hbm, tgt_hbm, ws_ref, wn_ref, b1_hbm, w2_hbm, b2_hbm,
    out_ref,
    feat_ref, req_ref, nbr_ref, tgt_ref, b1_ref, w2_ref, b2_ref,
    table, req_out, far_req, near_req, far_out, far_in, near_out, near_in, far_count, near_count,
    nbr_in, his, los, far_sum, near_sum, far_send, opposite_sum,
    w_own, w_nbr, w2_all, bias_out, bias_in, own_out, own_in, mean_out, mean_in, pre_own, y_out, y_in,
    req_ss, far_req_rs, near_req_rs, far_ss, far_rs, near_ss, near_rs, pair_ss, pair_rs,
    in_sem, w_sem, up_ss, up_rs, down_ss, down_rs, on_ss, on_rs, group_ss, group_rs,
):
    ring_x, ring_z, groups, own_rows, targets, cols = sizes
    nodes, chips = ring_x * ring_z, groups // 2
    blocks, part = own_rows // 256, targets // groups // 2
    hidden = groups * 64
    node, feat = lax.axis_index("node"), lax.axis_index("feat")
    my_x, my_z = lax.div(node, ring_z), lax.rem(node, ring_z)
    core = lax.bitwise_and(feat, 1)
    chip = lax.shift_right_logical(feat, 1)
    half = ring_z // 2
    far_reach, near_reach = lists(ring_z)
    far_steps, near_steps = 2 * far_reach + 1, 2 * near_reach + 1
    far_all, near_all = far_steps * ring_x, near_steps * ring_x
    far_self, near_self = far_all - ring_x, near_all - ring_x

    def at(dx, dz):
        z = my_z + dz
        z = jnp.where(z < 0, z + ring_z, jnp.where(z >= ring_z, z - ring_z, z))
        return lax.bitwise_and(my_x + ring_x + dx, ring_x - 1) * ring_z + z

    def place(p, steps):
        if isinstance(p, int):
            step = steps - 1 - p // ring_x
            return p % ring_x, (step + 1) // 2 * (1 if step % 2 else -1)
        step = steps - 1 - lax.shift_right_logical(p, ring_x.bit_length() - 1)
        ahead = lax.shift_right_logical(step + 1, 1)
        return lax.bitwise_and(p, ring_x - 1), jnp.where(lax.bitwise_and(step, 1) == 1, ahead, -ahead)

    def mate(k):
        return lax.bitwise_and(feat + k, groups - 1)

    def copy_to(axis, peer, src, dst, ss, rs):
        return pltpu.make_async_remote_copy(
            src_ref=src, dst_ref=dst, send_sem=ss, recv_sem=rs,
            device_id={axis: peer}, device_id_type=MESH,
        )

    def loop(low, high, body):
        def step(k, carry):
            body(k)
            return carry

        lax.fori_loop(low, high, step, 0)

    arrivals = [
        pltpu.make_async_copy(src, dst, in_sem.at[i])
        for i, (src, dst) in enumerate((
            (req_hbm, req_ref), (nbr_hbm, nbr_ref), (feat_hbm, feat_ref), (w2_hbm, w2_ref),
            (tgt_hbm, tgt_ref), (b1_hbm, b1_ref), (b2_hbm, b2_ref)))]
    for copy in arrivals:
        copy.start()

    barrier = pltpu.get_barrier_semaphore()
    for dz in sorted(range(ring_z), key=lambda z: -min(z, ring_z - z)):
        for dx in range(ring_x):
            if dx or dz:
                pl.semaphore_signal(barrier, inc=1, device_id={"node": at(dx, dz)}, device_id_type=MESH)
    for k in range(1, groups):
        pl.semaphore_signal(barrier, inc=1, device_id={"feat": mate(k)}, device_id_type=MESH)

    w_copies = [
        pltpu.make_async_copy(src, dst.at[:, pl.ds(0, cols), :], w_sem.at[i])
        for i, (src, dst) in enumerate(((ws_ref, w_own), (wn_ref, w_nbr)))]
    arrivals[0].wait()
    for j in range(nodes):
        req_out[j] = req_ref[pl.ds(j, 1), :]
    for copy in arrivals[1:]:
        copy.wait()

    pl.semaphore_wait(barrier, nodes - 1 + groups - 1)

    opposite = at(0, half)
    nbr_copy = copy_to("node", opposite, nbr_ref, nbr_in, pair_ss.at[0], pair_rs.at[0])
    sum_copy = copy_to("node", opposite, far_send, opposite_sum, pair_ss.at[1], pair_rs.at[1])
    for p in range(far_all):
        dx, dz = place(p, far_steps)
        owner = at(-dx, half - dz)
        copy_to("node", owner, req_out.at[owner], far_req.at[p], req_ss, far_req_rs.at[p // ring_x]).start()
    nbr_copy.start()
    for p in range(near_all):
        if p != near_self:
            dx, dz = place(p, near_steps)
            owner = at(-dx, -dz)
            copy_to("node", owner, req_out.at[owner], near_req.at[p], req_ss, near_req_rs.at[p // ring_x]).start()
    near_req[near_self] = req_out[node]

    for copy in w_copies:
        copy.start()
    for j in range(blocks):
        table[pl.ds(j * cols, cols), :] = feat_ref[:, pl.ds(j * 256, 256)]
    bias_out[...] = jnp.zeros_like(bias_out)
    bias_out[pl.ds(0, 1), pl.ds(0, 64)] = b1_ref[...]
    bias_out[pl.ds(1, 1), pl.ds(0, 64)] = b2_ref[...]
    bias_out[...] = bias_out[...] + pltpu.roll(bias_out[...], 64, 1)
    bias_in[0] = bias_out[...]

    ups, downs = chips // 2, (chips - 1) // 2

    def up(step):
        slot = w2_all.at[core, lax.bitwise_and(chip - step + chips, chips - 1)]
        return copy_to("feat", mate(2), slot if step else w2_ref, slot, up_ss.at[step], up_rs.at[step])

    def down(step):
        slot = w2_all.at[core, lax.bitwise_and(chip + step, chips - 1)]
        return copy_to("feat", mate(groups - 2), slot if step else w2_ref, slot, down_ss.at[step], down_rs.at[step])

    def pass_on(step):
        for copy, steps in ((up, ups), (down, downs)):
            if 0 < step <= steps:
                copy(step - 1).wait_recv()
            if step < steps:
                copy(step).start()

    w2_all[core, chip] = w2_ref[...]
    pass_on(0)

    def to_mates(src, dst, which):
        for k in sorted(range(1, groups), key=lambda k: -min(k, groups - k)):
            peer = mate(k)
            copy_to("feat", peer, src(peer), dst.at[k], group_ss.at[which], group_rs.at[which]).start()

    def from_mates(dst, which):
        rest = dst.at[pl.ds(1, groups - 1)]
        return copy_to("feat", mate(1), rest, rest, group_ss.at[which], group_rs.at[which])

    spread = jnp.where(
        lax.bitwise_and(lax.broadcasted_iota(jnp.int32, (FAN, 256), 1), 31)
        == lax.broadcasted_iota(jnp.int32, (FAN, 256), 0), 1.0, 0.0).astype(BF16)

    def spread_slots(slots, which):
        hi = lax.shift_right_logical(slots, 8).astype(F32).astype(BF16)
        lo = lax.bitwise_and(slots, 255).astype(F32).astype(BF16)
        his[which] = lax.dot_general(hi, spread, TN, preferred_element_type=F32)
        los[which] = lax.dot_general(lo, spread, TN, preferred_element_type=F32)

    def count_eight(which, owners, first):
        lane = lax.broadcasted_iota(jnp.int32, (8, 256), 1)
        sub = lax.broadcasted_iota(jnp.int32, (8, 256), 0)
        mine = (lax.shift_right_logical(lane, 5) == sub) & (lax.bitwise_and(lane, 31) < FAN)
        rows = pl.ds(pl.multiple_of(first, 8), 8)
        hi = jnp.where(mine, his[which, rows, :], -1.0)
        lo = jnp.sum(jnp.where(mine, los[which, rows, :], 0.0), axis=0, keepdims=True)
        left = jnp.concatenate([jnp.where(hi == owner, 1.0, 0.0) for owner in owners], axis=0)
        row = lax.broadcasted_iota(jnp.int32, (256, 256), 0)
        right = jnp.where(row == lo.astype(jnp.int32), 1.0, 0.0)
        both = lax.dot_general(left.astype(BF16), right.astype(BF16), NT, preferred_element_type=F32)
        return both.reshape(len(owners), 8, 256)

    def count_some(which, count, steps, low, high):
        owners = []
        for p in range(steps * ring_x):
            dx, dz = place(p, steps)
            owners.append(at(-dx, -dz).astype(F32))

        def body(k):
            for turn in range(UNROLL):
                first = pl.multiple_of((k * UNROLL + turn) * 16, 16)
                both = [count_eight(which, owners, first + 8 * i) for i in range(2)]
                count[:, pl.ds(first, 16), :] = jnp.concatenate(both, axis=1).astype(BF16)

        loop(low, high, body)

    turns = targets // (16 * UNROLL)
    early = min(EARLY, turns)
    spread_slots(nbr_ref[...], 0)
    count_some(0, near_count, near_steps, 0, early)

    def pick(index):
        block, within = lax.shift_right_logical(index, 8), lax.bitwise_and(index, 255)
        row = lax.broadcasted_iota(jnp.int32, (256, 256), 0)
        one_hot = jnp.where(row == within, 1.0, 0.0).astype(BF16)
        every = jnp.dot(table[...], one_hot, preferred_element_type=F32)
        found = every[0:cols]
        for j in range(1, blocks):
            found = jnp.where(block == j, every[j * cols:(j + 1) * cols], found)
        return found

    def span(refs, first, size):
        return refs.at[pl.ds(first, size)]

    def arrive(refs, sems, first, size, group):
        rest = span(refs, first, size)
        copy_to("node", opposite, rest, rest, req_ss, sems.at[group]).wait_recv()

    def serve(req, req_rs, out, into, ss, rs, steps, group, entries):
        arrive(req, req_rs, entries[0], len(entries), group)
        for p in entries:
            out[p] = pick(req[p]).astype(BF16)
        for p in entries:
            dx, dz = place(p, steps)
            copy_to("node", at(dx, dz), out.at[p], into.at[p], ss, rs.at[group]).start()

    loop(0, far_steps - 1, lambda g: serve(
        far_req, far_req_rs, far_out, far_in, far_ss, far_rs, far_steps, g,
        [ring_x * g + j for j in range(ring_x)]))
    arrive(far_req, far_req_rs, far_self, ring_x, far_steps - 1)
    for p in range(far_self, far_all):
        found = pick(far_req[p]).astype(BF16)
        if p == far_self:
            far_in[p] = found
        else:
            far_out[p] = found
            dx, dz = place(p, far_steps)
            copy_to("node", at(dx, dz), far_out.at[p], far_in.at[p], far_ss, far_rs.at[far_steps - 1]).start()
    pass_on(1)
    loop(0, near_steps - 1, lambda g: serve(
        near_req, near_req_rs, near_out, near_in, near_ss, near_rs, near_steps, g,
        [ring_x * g + j for j in range(ring_x)]))
    serve(near_req, near_req_rs, near_out, near_in, near_ss, near_rs, near_steps, near_steps - 1,
          list(range(near_self + 1, near_all)))
    near_in[near_self] = pick(near_req[near_self]).astype(BF16)
    pass_on(2)

    nbr_copy.wait_recv()
    spread_slots(nbr_in[...], 1)
    count_some(1, far_count, far_steps, 0, turns)

    def add_rows(total, count, rows, entries):
        for p in entries:
            total = total + lax.dot_general(rows[p], count[p], NT, preferred_element_type=F32)
        return total

    def take(rows, rs, count, sums, group, entries):
        arrive(rows, rs, entries[0], len(entries), group)
        sums[...] = add_rows(sums[...], count, rows, entries)

    def take_all(rows, rs, count, sums, steps):
        own = (steps - 1) * ring_x
        sums[...] = add_rows(jnp.zeros_like(sums), count, rows, [own])
        loop(0, steps - 1, lambda g: take(rows, rs, count, sums, g, [ring_x * g + j for j in range(ring_x)]))
        take(rows, rs, count, sums, steps - 1, list(range(own + 1, own + ring_x)))

    take_all(far_in, far_rs, far_count, far_sum, far_steps)
    far_send[...] = far_sum[...].astype(PARTIAL)
    sum_copy.start()
    pass_on(3)

    def pack(turned):
        gap = jnp.zeros((64 - cols, targets // 2), F32)
        return jnp.concatenate(
            [turned[:, :targets // 2], gap, turned[:, targets // 2:], gap], axis=0).T.astype(BF16)

    def share_of(ref):
        return lambda peer: ref.at[pl.ds(pl.multiple_of(peer * part, part), part), :]

    def unpack(ref):
        tiles = [ref[lax.bitwise_and(feat - j + groups, groups - 1)] for j in range(groups)]
        top = jnp.concatenate(tiles, axis=1)
        rolled = [pltpu.roll(tile.astype(F32), 64, 1).astype(BF16) for tile in tiles]
        return jnp.concatenate([top, jnp.concatenate(rolled, axis=1)], axis=0)

    own = jnp.concatenate([pick(tgt_ref[:, pl.ds(j * 256, 256)]) for j in range(targets // 256)], axis=1)
    own_out[...] = pack(own)
    own_in[0] = own_out[pl.ds(pl.multiple_of(feat * part, part), part), :]
    to_mates(share_of(own_out), own_in, 0)
    to_mates(lambda peer: bias_out, bias_in, 1)

    count_some(0, near_count, near_steps, early, turns)
    take_all(near_in, near_rs, near_count, near_sum, near_steps)

    pass_on(4)
    side = copy_to("feat", feat + 1 - 2 * core, w2_all.at[core], w2_all.at[core], on_ss, on_rs)
    side.start()

    for copy, weight in zip(w_copies, (w_own, w_nbr), strict=True):
        weight[:, pl.ds(cols, 128 - cols), :] = jnp.zeros((groups, 128 - cols, hidden), BF16)
        copy.wait()
    from_mates(own_in, 0).wait_recv()
    from_mates(bias_in, 1).wait_recv()
    low_half = lax.broadcasted_iota(jnp.int32, (1, 128), 1) < 64

    def bias_row(row, order):
        def of(g):
            return bias_in[lax.bitwise_and(feat - g + groups, groups - 1), pl.ds(row, 1), :]

        pairs = zip(order[::2], order[1::2], strict=True)
        return jnp.concatenate([jnp.where(low_half, of(a), of(b)) for a, b in pairs], axis=1)

    by_core = [2 * j + c for c in range(2) for j in range(chips)]
    second_bias = bias_row(1, by_core)
    pre_own[...] = jnp.dot(
        unpack(own_in), w_own[...].reshape(groups * 128, hidden), preferred_element_type=F32,
    ) + bias_row(0, list(range(groups)))

    def sent(refs, size, sem):
        rest = span(refs, 0, size)
        copy_to("node", opposite, rest, rest, sem, pair_rs.at[0]).wait_send()

    sent(req_out, nodes - 1, req_ss)
    sent(far_out, far_all - 1, far_ss)
    sent(near_out, near_all - 1, near_ss)
    nbr_copy.wait_send()
    for copy, steps in ((up, ups), (down, downs)):
        for step in range(steps):
            copy(step).wait_send()
    from_mates(own_in, 0).wait_send()
    from_mates(bias_in, 1).wait_send()

    sum_copy.wait_recv()
    mean_out[...] = pack((near_sum[...] + opposite_sum[...].astype(F32)) / FAN)
    to_mates(share_of(mean_out), mean_in, 2)
    mean_in[0] = mean_out[pl.ds(pl.multiple_of(feat * part, part), part), :]
    sum_copy.wait_send()
    side.wait_send()
    other = w2_all.at[1 - core]
    copy_to("feat", feat + 1 - 2 * core, other, other, on_ss, on_rs).wait_recv()
    from_mates(mean_in, 2).wait_recv()

    pre = pre_own[...] + jnp.dot(
        unpack(mean_in), w_nbr[...].reshape(groups * 128, hidden), preferred_element_type=F32)
    one = jnp.maximum(pre, 0.0).astype(BF16)
    two = lax.dot_general(one, w2_all[...].reshape(hidden, hidden), NT, preferred_element_type=F32) + second_bias
    for j in range(groups // 2):
        above, below = two[:part, j * 128:(j + 1) * 128], two[part:, j * 128:(j + 1) * 128]
        y_out[2 * j] = jnp.where(low_half, above, pltpu.roll(below, 64, 1)).astype(BF16)
        y_out[2 * j + 1] = jnp.where(low_half, pltpu.roll(above, 64, 1), below).astype(BF16)

    def rank(peer):
        return lax.bitwise_and(peer, 1) * chips + lax.shift_right_logical(peer, 1)

    to_mates(lambda peer: y_out.at[rank(peer)], y_in, 3)
    y_in[0] = y_out[rank(feat)]
    from_mates(mean_in, 2).wait_send()
    from_mates(y_in, 3).wait_recv()
    shares = [y_in[lax.bitwise_and(feat - j + groups, groups - 1)] for j in range(groups)]
    turned = jnp.concatenate(shares, axis=0).astype(F32).T
    out_ref[...] = jnp.concatenate([turned[0:64], turned[64:128]], axis=1).astype(BF16)
    from_mates(y_in, 3).wait_send()


def local(groups, ring_x, features, req_local, nbr_slot, target_ids, w_self, w_neigh, bias_one, w_two, bias_two):
    _, nodes, cap = req_local.shape
    own_rows, cols = features.shape
    targets, fan = nbr_slot.shape
    hidden = w_self.shape[1]
    part, chips = targets // groups // 2, groups // 2
    sizes = (ring_x, nodes // ring_x, groups, own_rows, targets, cols)
    far_steps, near_steps = (2 * reach + 1 for reach in lists(nodes // ring_x))
    far, near = far_steps * ring_x, near_steps * ring_x
    vmem = pl.BlockSpec(memory_space=pltpu.VMEM)
    hbm = pl.BlockSpec(memory_space=pl.ANY)
    dma = pltpu.SemaphoreType.DMA
    out = pl.pallas_call(
        functools.partial(kernel, sizes),
        out_shape=jax.ShapeDtypeStruct((64, targets), BF16),
        in_specs=[hbm] * 9,
        out_specs=vmem,
        scratch_shapes=[
            pltpu.VMEM((cols, own_rows), BF16),
            pltpu.VMEM((nodes, cap), jnp.int32),
            pltpu.VMEM((fan, targets), jnp.int32),
            pltpu.VMEM((1, targets), jnp.int32),
            pltpu.VMEM((1, 64), F32),
            pltpu.VMEM((64, hidden), BF16),
            pltpu.VMEM((1, 64), F32),
            pltpu.VMEM((own_rows // 256 * cols, 256), BF16),
            pltpu.VMEM((nodes, 1, cap), jnp.int32),
            pltpu.VMEM((far, 1, cap), jnp.int32),
            pltpu.VMEM((near, 1, cap), jnp.int32),
            pltpu.VMEM((far, cols, cap), BF16),
            pltpu.VMEM((far, cols, cap), BF16),
            pltpu.VMEM((near, cols, cap), BF16),
            pltpu.VMEM((near, cols, cap), BF16),
            pltpu.VMEM((far, targets, cap), BF16),
            pltpu.VMEM((near, targets, cap), BF16),
            pltpu.VMEM((fan, targets), jnp.int32),
            pltpu.VMEM((2, targets, 256), F32),
            pltpu.VMEM((2, targets, 256), F32),
            pltpu.VMEM((cols, targets), F32),
            pltpu.VMEM((cols, targets), F32),
            pltpu.VMEM((cols, targets), PARTIAL),
            pltpu.VMEM((cols, targets), PARTIAL),
            pltpu.VMEM((groups, 128, hidden), BF16),
            pltpu.VMEM((groups, 128, hidden), BF16),
            pltpu.VMEM((2, chips, 64, hidden), BF16),
            pltpu.VMEM((8, 128), F32),
            pltpu.VMEM((groups, 8, 128), F32),
            pltpu.VMEM((targets // 2, 128), BF16),
            pltpu.VMEM((groups, part, 128), BF16),
            pltpu.VMEM((targets // 2, 128), BF16),
            pltpu.VMEM((groups, part, 128), BF16),
            pltpu.VMEM((2 * part, hidden), F32),
            pltpu.VMEM((groups, part, 128), BF16),
            pltpu.VMEM((groups, part, 128), BF16),
            dma(()), dma((far_steps,)), dma((near_steps,)),
            dma(()), dma((far_steps,)), dma(()), dma((near_steps,)), dma((2,)), dma((2,)),
            dma((7,)), dma((2,)), dma((4,)), dma((4,)), dma((4,)), dma((4,)), dma(()), dma(()), dma((4,)), dma((4,)),
        ],
        compiler_params=pltpu.CompilerParams(
            collective_id=0, has_side_effects=True, vmem_limit_bytes=56 * 1024 * 1024
        ),
    )(
        features.T, req_local[0], nbr_slot.T, target_ids[None, :],
        w_self.reshape(groups, cols, hidden), w_neigh.reshape(groups, cols, hidden),
        bias_one[None, :], w_two.T, bias_two[None, :],
    )
    return out.T


def solution(mesh):
    placed = (
        P("node", "feat"),
        P("node", None, None),
        P("node", None),
        P("node"),
        P(),
        P(),
        P("feat"),
        P(None, "feat"),
        P("feat"),
    )
    return jax.shard_map(
        functools.partial(local, mesh.shape["feat"], RING_X), mesh=mesh, in_specs=placed,
        out_specs=P("node", "feat"), check_vma=False,
    )
```

time: 298 us -> 66.6 us (0.22)
  waiting for transfers between devices: 155 us -> 0 us
  local copies, waits for them, and re-layouts: 90 us -> 1.47 us
  Pallas kernels: 0 us -> 65 us
  starting transfers between devices: 24.4 us -> 0 us
  between operations: 13.5 us -> 0.01 us
  matrix products: 7.68 us -> 0 us
  other arithmetic: 6.86 us -> 0 us
    gather x4 -> x0, local copies, waits for them, and re-layouts: 75.6 us -> none  [the longest x2 47.7 us: local(): lookup = features[served]]
    pallas_call x0 -> x1, Pallas kernels: none -> 65 us  [local(): pl.pallas_call(functools.partial(kernel, sizes), out_shape=jax.ShapeDtype...]
    unnamed x3 -> x0, waiting for transfers between devices: 64.2 us -> none
    all_to_all x2 -> x0, waiting for transfers between devices: 45.8 us -> none  [the longest x1 35.9 us: local(): lax.all_to_all(lookup, 'node', split_axis=0, concat_axis=0, tiled=True)]
    all_gather x1 -> x0, waiting for transfers between devices: 44.9 us -> none  [local(): lax.all_gather(hidden_one, 'feat', axis=1, tiled=True)]
    all_to_all x2 -> x0, starting transfers between devices: 24.3 us -> none  [the longest x1 18.8 us: local(): lax.all_to_all(wanted, 'node', split_axis=0, concat_axis=0, tiled=True)]
    dot_general x3 -> x0, matrix products: 7.68 us -> none  [the longest x1 3.59 us: local(): jnp.dot(neigh_mean, neigh_rows, preferred_element_type=jnp.float32)]
    convert_element_type x1 -> x0, local copies, waits for them, and re-layouts: 6.95 us -> none  [local(): picked = buffer[nbr_slot].astype(jnp.float32)]
  transfers between devices with their start and end apart: 4 -> 0, of which waited for: 4 -> 0; matrix products, arithmetic and copies ran while one was open for 2% -> 0% of each run, Pallas kernels for 0% -> 0%
where the time goes in v3:
time: 66.6 us; the launch traced here: 66.4 us
  Pallas kernels  65 us (98%)
  local copies, waits for them, and re-layouts  1.47 us (2%)
    pallas_call x1, Pallas kernels, local(): pl.pallas_call(functools.partial(kernel, sizes), out_shape=jax.ShapeDtype...  65 us
    unnamed x1, local copies, waits for them, and re-layouts  1.47 us

profile of v3, /device:TPU:1, one launch (start us, length us, event | category | flops | bytes accessed | tf_op | source)
XLA Modules:
  0.0 66.4 jit_solution(16729794916458093667)
XLA Ops:
  0.0 65.0 %shard_map.91 = bf16[64,512]{1,0:T(8,128)(2,1)} custom-call(bf16[48,4096]{1,0:T(8,128)(2,1)} %bitcast.12, s32[48,256]{1,0:T(8,128)} %bitcast.16, s32[25,512]{1,0:T(8,128)} %bitcast.15, s32[1,512]{1,0:T(1,128)} %bitcast.17, bf16[16,48,1024]{2,1,0:T(8,128)(2,1)} %bitcast.10, bf16[16,48,1024]{2,1,0:T(8,128)(2,1)} %bitcast.11, f32[1,64]{1,0:T(1,128)} %bitcast.18, ...), custom_call_target="tpu_custom_call" | custom-call | tf_op jit(solution)/shard_map/pallas_call | solution.py:379
  65.0 1.5 %copy.11 = bf16[512,64]{0,1:T(8,128)(2,1)} copy(bf16[512,64]{0,1:T(8,128)(2,1)} %bitcast.13) | data formatting | bytes 131072

commit v4 on v3

--- a/solution.py
+++ b/solution.py
@@ -24,13 +24,22 @@
     return far, ring_z // 2 - 1 - far
 
 
+def pair_up(numbers):
+    size = numbers.shape[1] // 2
+    return numbers[:, :size] + lax.shift_left(numbers[:, size:], 16)
+
+
+def take_apart(pairs):
+    return jnp.concatenate([lax.bitwise_and(pairs, 0xFFFF), lax.shift_right_logical(pairs, 16)], axis=1)
+
+
 def kernel(
     sizes,
     feat_hbm, req_hbm, nbr_hbm, tgt_hbm, ws_ref, wn_ref, b1_hbm, w2_hbm, b2_hbm,
     out_ref,
     feat_ref, req_ref, nbr_ref, tgt_ref, b1_ref, w2_ref, b2_ref,
     table, req_out, far_req, near_req, far_out, far_in, near_out, near_in, far_count, near_count,
-    nbr_in, his, los, far_sum, near_sum, far_send, opposite_sum,
+    nbr_send, nbr_in, his, los, far_sum, near_sum, far_send, opposite_sum,
     w_own, w_nbr, w2_all, bias_out, bias_in, own_out, own_in, mean_out, mean_in, pre_own, y_out, y_in,
     req_ss, far_req_rs, near_req_rs, far_ss, far_rs, near_ss, near_rs, pair_ss, pair_rs,
     in_sem, w_sem, up_ss, up_rs, down_ss, down_rs, on_ss, on_rs, group_ss, group_rs,
@@ -95,69 +104,15 @@
         pl.semaphore_signal(barrier, inc=1, device_id={"feat": mate(k)}, device_id_type=MESH)
 
     w_copies = [
-        pltpu.make_async_copy(src, dst.at[:, pl.ds(0, cols), :], w_sem.at[i])
+        pltpu.make_async_copy(src, dst.at[:, :, pl.ds(0, cols), :], w_sem.at[i])
         for i, (src, dst) in enumerate(((ws_ref, w_own), (wn_ref, w_nbr)))]
     arrivals[0].wait()
+    asked = pair_up(req_ref[...])
     for j in range(nodes):
-        req_out[j] = req_ref[pl.ds(j, 1), :]
+        req_out[j] = asked[j:j + 1]
     for copy in arrivals[1:]:
         copy.wait()
-
-    pl.semaphore_wait(barrier, nodes - 1 + groups - 1)
-
-    opposite = at(0, half)
-    nbr_copy = copy_to("node", opposite, nbr_ref, nbr_in, pair_ss.at[0], pair_rs.at[0])
-    sum_copy = copy_to("node", opposite, far_send, opposite_sum, pair_ss.at[1], pair_rs.at[1])
-    for p in range(far_all):
-        dx, dz = place(p, far_steps)
-        owner = at(-dx, half - dz)
-        copy_to("node", owner, req_out.at[owner], far_req.at[p], req_ss, far_req_rs.at[p // ring_x]).start()
-    nbr_copy.start()
-    for p in range(near_all):
-        if p != near_self:
-            dx, dz = place(p, near_steps)
-            owner = at(-dx, -dz)
-            copy_to("node", owner, req_out.at[owner], near_req.at[p], req_ss, near_req_rs.at[p // ring_x]).start()
-    near_req[near_self] = req_out[node]
-
-    for copy in w_copies:
-        copy.start()
-    for j in range(blocks):
-        table[pl.ds(j * cols, cols), :] = feat_ref[:, pl.ds(j * 256, 256)]
-    bias_out[...] = jnp.zeros_like(bias_out)
-    bias_out[pl.ds(0, 1), pl.ds(0, 64)] = b1_ref[...]
-    bias_out[pl.ds(1, 1), pl.ds(0, 64)] = b2_ref[...]
-    bias_out[...] = bias_out[...] + pltpu.roll(bias_out[...], 64, 1)
-    bias_in[0] = bias_out[...]
-
-    ups, downs = chips // 2, (chips - 1) // 2
-
-    def up(step):
-        slot = w2_all.at[core, lax.bitwise_and(chip - step + chips, chips - 1)]
-        return copy_to("feat", mate(2), slot if step else w2_ref, slot, up_ss.at[step], up_rs.at[step])
-
-    def down(step):
-        slot = w2_all.at[core, lax.bitwise_and(chip + step, chips - 1)]
-        return copy_to("feat", mate(groups - 2), slot if step else w2_ref, slot, down_ss.at[step], down_rs.at[step])
-
-    def pass_on(step):
-        for copy, steps in ((up, ups), (down, downs)):
-            if 0 < step <= steps:
-                copy(step - 1).wait_recv()
-            if step < steps:
-                copy(step).start()
-
-    w2_all[core, chip] = w2_ref[...]
-    pass_on(0)
-
-    def to_mates(src, dst, which):
-        for k in sorted(range(1, groups), key=lambda k: -min(k, groups - k)):
-            peer = mate(k)
-            copy_to("feat", peer, src(peer), dst.at[k], group_ss.at[which], group_rs.at[which]).start()
-
-    def from_mates(dst, which):
-        rest = dst.at[pl.ds(1, groups - 1)]
-        return copy_to("feat", mate(1), rest, rest, group_ss.at[which], group_rs.at[which])
+    nbr_send[...] = pair_up(nbr_ref[...])
 
     spread = jnp.where(
         lax.bitwise_and(lax.broadcasted_iota(jnp.int32, (FAN, 256), 1), 31)
@@ -201,6 +156,62 @@
     spread_slots(nbr_ref[...], 0)
     count_some(0, near_count, near_steps, 0, early)
 
+    pl.semaphore_wait(barrier, nodes - 1 + groups - 1)
+
+    opposite = at(0, half)
+    nbr_copy = copy_to("node", opposite, nbr_send, nbr_in, pair_ss.at[0], pair_rs.at[0])
+    sum_copy = copy_to("node", opposite, far_send, opposite_sum, pair_ss.at[1], pair_rs.at[1])
+    for p in range(far_all):
+        dx, dz = place(p, far_steps)
+        owner = at(-dx, half - dz)
+        copy_to("node", owner, req_out.at[owner], far_req.at[p], req_ss, far_req_rs.at[p // ring_x]).start()
+    for p in range(near_all):
+        if p != near_self:
+            dx, dz = place(p, near_steps)
+            owner = at(-dx, -dz)
+            copy_to("node", owner, req_out.at[owner], near_req.at[p], req_ss, near_req_rs.at[p // ring_x]).start()
+    near_req[near_self] = req_out[node]
+    nbr_copy.start()
+
+    for copy in w_copies:
+        copy.start()
+    for j in range(blocks):
+        table[pl.ds(j * cols, cols), :] = feat_ref[:, pl.ds(j * 256, 256)]
+    bias_out[...] = jnp.zeros_like(bias_out)
+    bias_out[pl.ds(0, 1), pl.ds(0, 64)] = b1_ref[...]
+    bias_out[pl.ds(1, 1), pl.ds(0, 64)] = b2_ref[...]
+    bias_out[...] = bias_out[...] + pltpu.roll(bias_out[...], 64, 1)
+    bias_in[0] = bias_out[...]
+
+    ups, downs = chips // 2, (chips - 1) // 2
+
+    def up(step):
+        slot = w2_all.at[core, lax.bitwise_and(chip - step + chips, chips - 1)]
+        return copy_to("feat", mate(2), slot if step else w2_ref, slot, up_ss.at[step], up_rs.at[step])
+
+    def down(step):
+        slot = w2_all.at[core, lax.bitwise_and(chip + step, chips - 1)]
+        return copy_to("feat", mate(groups - 2), slot if step else w2_ref, slot, down_ss.at[step], down_rs.at[step])
+
+    def pass_on(step):
+        for copy, steps in ((up, ups), (down, downs)):
+            if 0 < step <= steps:
+                copy(step - 1).wait_recv()
+            if step < steps:
+                copy(step).start()
+
+    w2_all[core, chip] = w2_ref[...]
+    pass_on(0)
+
+    def to_mates(src, dst, which):
+        for k in sorted(range(1, groups), key=lambda k: -min(k, groups - k)):
+            peer = mate(k)
+            copy_to("feat", peer, src(peer), dst.at[k], group_ss.at[which], group_rs.at[which]).start()
+
+    def from_mates(dst, which):
+        rest = dst.at[pl.ds(1, groups - 1)]
+        return copy_to("feat", mate(1), rest, rest, group_ss.at[which], group_rs.at[which])
+
     def pick(index):
         block, within = lax.shift_right_logical(index, 8), lax.bitwise_and(index, 255)
         row = lax.broadcasted_iota(jnp.int32, (256, 256), 0)
@@ -221,7 +232,7 @@
     def serve(req, req_rs, out, into, ss, rs, steps, group, entries):
         arrive(req, req_rs, entries[0], len(entries), group)
         for p in entries:
-            out[p] = pick(req[p]).astype(BF16)
+            out[p] = pick(take_apart(req[p])).astype(BF16)
         for p in entries:
             dx, dz = place(p, steps)
             copy_to("node", at(dx, dz), out.at[p], into.at[p], ss, rs.at[group]).start()
@@ -231,7 +242,7 @@
         [ring_x * g + j for j in range(ring_x)]))
     arrive(far_req, far_req_rs, far_self, ring_x, far_steps - 1)
     for p in range(far_self, far_all):
-        found = pick(far_req[p]).astype(BF16)
+        found = pick(take_apart(far_req[p])).astype(BF16)
         if p == far_self:
             far_in[p] = found
         else:
@@ -244,11 +255,11 @@
         [ring_x * g + j for j in range(ring_x)]))
     serve(near_req, near_req_rs, near_out, near_in, near_ss, near_rs, near_steps, near_steps - 1,
           list(range(near_self + 1, near_all)))
-    near_in[near_self] = pick(near_req[near_self]).astype(BF16)
+    near_in[near_self] = pick(take_apart(near_req[near_self])).astype(BF16)
     pass_on(2)
 
     nbr_copy.wait_recv()
-    spread_slots(nbr_in[...], 1)
+    spread_slots(take_apart(nbr_in[...]), 1)
     count_some(1, far_count, far_steps, 0, turns)
 
     def add_rows(total, count, rows, entries):
@@ -279,11 +290,15 @@
     def share_of(ref):
         return lambda peer: ref.at[pl.ds(pl.multiple_of(peer * part, part), part), :]
 
+    low_half = lax.broadcasted_iota(jnp.int32, (1, 128), 1) < 64
+
     def unpack(ref):
-        tiles = [ref[lax.bitwise_and(feat - j + groups, groups - 1)] for j in range(groups)]
-        top = jnp.concatenate(tiles, axis=1)
-        rolled = [pltpu.roll(tile.astype(F32), 64, 1).astype(BF16) for tile in tiles]
-        return jnp.concatenate([top, jnp.concatenate(rolled, axis=1)], axis=0)
+        tiles = [ref[lax.bitwise_and(feat - j + groups, groups - 1)].astype(F32) for j in range(groups)]
+        tops, bottoms = [], []
+        for left, right in zip(tiles[::2], tiles[1::2], strict=True):
+            tops.append(jnp.where(low_half, left, pltpu.roll(right, 64, 1)).astype(BF16))
+            bottoms.append(jnp.where(low_half, pltpu.roll(left, 64, 1), right).astype(BF16))
+        return jnp.concatenate([jnp.concatenate(tops, axis=1), jnp.concatenate(bottoms, axis=1)], axis=0)
 
     own = jnp.concatenate([pick(tgt_ref[:, pl.ds(j * 256, 256)]) for j in range(targets // 256)], axis=1)
     own_out[...] = pack(own)
@@ -292,18 +307,15 @@
     to_mates(lambda peer: bias_out, bias_in, 1)
 
     count_some(0, near_count, near_steps, early, turns)
-    take_all(near_in, near_rs, near_count, near_sum, near_steps)
-
     pass_on(4)
     side = copy_to("feat", feat + 1 - 2 * core, w2_all.at[core], w2_all.at[core], on_ss, on_rs)
     side.start()
 
     for copy, weight in zip(w_copies, (w_own, w_nbr), strict=True):
-        weight[:, pl.ds(cols, 128 - cols), :] = jnp.zeros((groups, 128 - cols, hidden), BF16)
+        weight[:, :, pl.ds(cols, 64 - cols), :] = jnp.zeros((chips, 2, 64 - cols, hidden), BF16)
         copy.wait()
     from_mates(own_in, 0).wait_recv()
     from_mates(bias_in, 1).wait_recv()
-    low_half = lax.broadcasted_iota(jnp.int32, (1, 128), 1) < 64
 
     def bias_row(row, order):
         def of(g):
@@ -315,8 +327,10 @@
     by_core = [2 * j + c for c in range(2) for j in range(chips)]
     second_bias = bias_row(1, by_core)
     pre_own[...] = jnp.dot(
-        unpack(own_in), w_own[...].reshape(groups * 128, hidden), preferred_element_type=F32,
+        unpack(own_in), w_own[...].reshape(groups * 64, hidden), preferred_element_type=F32,
     ) + bias_row(0, list(range(groups)))
+
+    take_all(near_in, near_rs, near_count, near_sum, near_steps)
 
     def sent(refs, size, sem):
         rest = span(refs, 0, size)
@@ -324,7 +338,6 @@
 
     sent(req_out, nodes - 1, req_ss)
     sent(far_out, far_all - 1, far_ss)
-    sent(near_out, near_all - 1, near_ss)
     nbr_copy.wait_send()
     for copy, steps in ((up, ups), (down, downs)):
         for step in range(steps):
@@ -337,13 +350,14 @@
     to_mates(share_of(mean_out), mean_in, 2)
     mean_in[0] = mean_out[pl.ds(pl.multiple_of(feat * part, part), part), :]
     sum_copy.wait_send()
+    sent(near_out, near_all - 1, near_ss)
     side.wait_send()
     other = w2_all.at[1 - core]
     copy_to("feat", feat + 1 - 2 * core, other, other, on_ss, on_rs).wait_recv()
     from_mates(mean_in, 2).wait_recv()
 
     pre = pre_own[...] + jnp.dot(
-        unpack(mean_in), w_nbr[...].reshape(groups * 128, hidden), preferred_element_type=F32)
+        unpack(mean_in), w_nbr[...].reshape(groups * 64, hidden), preferred_element_type=F32)
     one = jnp.maximum(pre, 0.0).astype(BF16)
     two = lax.dot_general(one, w2_all[...].reshape(hidden, hidden), NT, preferred_element_type=F32) + second_bias
     for j in range(groups // 2):
@@ -390,24 +404,25 @@
             pltpu.VMEM((64, hidden), BF16),
             pltpu.VMEM((1, 64), F32),
             pltpu.VMEM((own_rows // 256 * cols, 256), BF16),
-            pltpu.VMEM((nodes, 1, cap), jnp.int32),
-            pltpu.VMEM((far, 1, cap), jnp.int32),
-            pltpu.VMEM((near, 1, cap), jnp.int32),
+            pltpu.VMEM((nodes, 1, cap // 2), jnp.int32),
+            pltpu.VMEM((far, 1, cap // 2), jnp.int32),
+            pltpu.VMEM((near, 1, cap // 2), jnp.int32),
             pltpu.VMEM((far, cols, cap), BF16),
             pltpu.VMEM((far, cols, cap), BF16),
             pltpu.VMEM((near, cols, cap), BF16),
             pltpu.VMEM((near, cols, cap), BF16),
             pltpu.VMEM((far, targets, cap), BF16),
             pltpu.VMEM((near, targets, cap), BF16),
-            pltpu.VMEM((fan, targets), jnp.int32),
+            pltpu.VMEM((fan, targets // 2), jnp.int32),
+            pltpu.VMEM((fan, targets // 2), jnp.int32),
             pltpu.VMEM((2, targets, 256), F32),
             pltpu.VMEM((2, targets, 256), F32),
             pltpu.VMEM((cols, targets), F32),
             pltpu.VMEM((cols, targets), F32),
             pltpu.VMEM((cols, targets), PARTIAL),
             pltpu.VMEM((cols, targets), PARTIAL),
-            pltpu.VMEM((groups, 128, hidden), BF16),
-            pltpu.VMEM((groups, 128, hidden), BF16),
+            pltpu.VMEM((chips, 2, 64, hidden), BF16),
+            pltpu.VMEM((chips, 2, 64, hidden), BF16),
             pltpu.VMEM((2, chips, 64, hidden), BF16),
             pltpu.VMEM((8, 128), F32),
             pltpu.VMEM((groups, 8, 128), F32),
@@ -427,7 +442,7 @@
         ),
     )(
         features.T, req_local[0], nbr_slot.T, target_ids[None, :],
-        w_self.reshape(groups, cols, hidden), w_neigh.reshape(groups, cols, hidden),
+        w_self.reshape(chips, 2, cols, hidden), w_neigh.reshape(chips, 2, cols, hidden),
         bias_one[None, :], w_two.T, bias_two[None, :],
     )
     return out.T

time: 66.6 us -> 66.7 us (level)
  no operation moved by 1% of the time
where the time goes in v4:
time: 66.7 us; the launch traced here: 66.6 us
  Pallas kernels  65.1 us (98%)
  local copies, waits for them, and re-layouts  1.47 us (2%)
    pallas_call x1, Pallas kernels, local(): pl.pallas_call(functools.partial(kernel, sizes), out_shape=jax.ShapeDtype...  65.1 us
    unnamed x1, local copies, waits for them, and re-layouts  1.47 us

profile of v4, /device:TPU:1, one launch (start us, length us, event | category | flops | bytes accessed | tf_op | source)
XLA Modules:
  0.0 66.6 jit_solution(3703447581888012462)
XLA Ops:
  0.0 65.1 %shard_map.91 = bf16[64,512]{1,0:T(8,128)(2,1)} custom-call(bf16[48,4096]{1,0:T(8,128)(2,1)} %bitcast.12, s32[48,256]{1,0:T(8,128)} %bitcast.16, s32[25,512]{1,0:T(8,128)} %bitcast.15, s32[1,512]{1,0:T(1,128)} %bitcast.17, bf16[8,2,48,1024]{3,2,1,0:T(8,128)(2,1)} %bitcast.10, bf16[8,2,48,1024]{3,2,1,0:T(8,128)(2,1)} %bitcast.11, f32[1,64]{1,0:T(1,128)} %bitcast.18, ...), custom_call_target="tpu_custom_call" | custom-call | tf_op jit(solution)/shard_map/pallas_call | solution.py:393
  65.1 1.5 %copy.11 = bf16[512,64]{0,1:T(8,128)(2,1)} copy(bf16[512,64]{0,1:T(8,128)(2,1)} %bitcast.13) | data formatting | bytes 131072
